TPU v7x, 256 devices: a whole 4x4x8 slice. The times are simulated.
256 devices in a mesh: row: 16 (over y_hi, x, core), col: 16 (over z, y_lo).
Axes of the slice: x: 4, y: 4 (y_hi: 2, y_lo: 2; y = y_hi * 2 + y_lo), z: 8, core: 2. Of those that a mesh axis runs over, the one named last changes fastest.
Arguments:
- integrals: bfloat16 [896, 32, 28672], P('row', 'col'), may hold values from -0.0068359375 to 0.0068359375
- amplitudes: bfloat16 [896, 917504], P('row', 'col'), may hold values from -6 to 6
Outputs:
- ladder_out: bfloat16 [32, 32, 32, 32], P('col', None, 'row')
All inputs are finite; a program needn't handle non-finite values.
Results may differ from a plain program's by a relative error of at most 0.0051.
Values may be sent and summed in bfloat16 or wider, within the bound.
A program may use at most 320 MiB of HBM per device.

v0:
```python
import jax
import jax.numpy as jnp
from jax import lax
from jax.sharding import PartitionSpec as P

NV = 896
VB = 32
OB = 32


def shards(integrals, amplitudes):
    row_count = lax.axis_size("row")
    col_count = lax.axis_size("col")
    first_width = integrals.shape[0]
    alpha_width = integrals.shape[1]
    block_width = VB
    virtual_count = NV
    second_width = virtual_count // col_count
    pair_count = OB * OB
    panels = lax.all_to_all(integrals, "col", split_axis=2, concat_axis=1, tiled=True)
    weights = panels.reshape(first_width, block_width, second_width, block_width)
    amp_block = amplitudes.reshape(first_width, second_width, pair_count)
    partial_value = lax.psum_scatter(
        jnp.einsum("cadb,cdp->abp", weights, amp_block, preferred_element_type=jnp.float32),
        "col",
        scatter_dimension=0,
        tiled=True,
    )
    summed = lax.psum_scatter(partial_value, "row", scatter_dimension=2, tiled=True)
    ladder = lax.optimization_barrier(summed.astype(jnp.bfloat16))
    ladder = ladder.reshape(alpha_width, block_width, OB // row_count, OB)
    returned = lax.all_to_all(
        lax.all_to_all(ladder, "row", split_axis=3, concat_axis=2, tiled=True),
        "col",
        split_axis=1,
        concat_axis=0,
        tiled=True,
    )
    mirror = jnp.transpose(returned, (1, 0, 3, 2))
    return (ladder.astype(jnp.float32) + mirror.astype(jnp.float32)).astype(jnp.bfloat16)


def solution(mesh):
    return jax.shard_map(
        shards,
        mesh=mesh,
        in_specs=(P("row", "col", None), P("row", "col")),
        out_specs=P("col", None, "row", None),
        check_vma=False,
    )
```

profile of v0, /device:TPU:1, one launch (start us, length us, event | category | flops | bytes accessed | tf_op | source)
XLA Modules:
  0.0 479.7 jit_solution(1707642739775911494)
XLA Ops:
  6.5 0.0 reduce-scatter.5.cloned.1.call-start
  6.5 36.6 %copy.38 = bf16[56,2,28672]{0,1,2:T(2,128)(2,1)} copy(bf16[56,2,28672]{2,1,0:T(2,128)(2,1)} %param.2) | data formatting | bytes 12845056 | tf_op args[0]
  43.1 27.0 %reshape.23 = bf16[16,2,100352]{2,1,0:T(2,128)(2,1)} reshape(bf16[28672,2,56]{2,1,0:T(2,128)(2,1)} %bitcast.42) | data formatting | bytes 12845056
  70.1 153.4 %all_to_all.42 = bf16[16,2,100352]{2,1,0:T(2,128)(2,1)} all-to-all(bf16[16,2,100352]{2,1,0:T(2,128)(2,1)} %reshape.23), channel_id=1, replica_groups=mesh['row'=16,'col'=16] {'col'}, dimensions={0} | all-to-all | bytes 12845056 | tf_op jit(solution)/shard_map/all_to_all | solution.py:20
  223.5 0.0 slice-start
  223.5 26.9 %reshape.24 = bf16[28672,2,56]{2,1,0:T(2,128)(2,1)} reshape(bf16[16,2,100352]{2,1,0:T(2,128)(2,1)} %all_to_all.42) | data formatting | bytes 12845056
  250.3 0.0 slice-start.1
  250.3 9.1 %copy.51 = bf16[56,2,16,1792]{0,3,1,2:T(8,128)(2,1)S(1)} copy(bf16[56,2,16,1792]{0,1,3,2:T(2,128)(2,1)} %bitcast.41) | data formatting | bytes 12845056 | tf_op jit(solution)/shard_map/all_to_all | solution.py:20
  259.5 0.0 slice-done
  259.5 0.0 slice-done.1
  259.5 9.7 %fusion.2 = f32[32,32,1024]{2,1,0:T(8,128)} fusion(bf16[56,32,56,32]{0,3,2,1:T(8,128)(2,1)S(1)} %bitcast.43, bf16[7,56,8,1024]{3,2,1,0:T(8,128)(2,1)S(1)} %bitcast.56), kind=kOutput, calls=%fused_computation.3 | convolution fusion | flops 6576668672 | bytes 17039360 | tf_op jit(solution)/shard_map/cadb,cdp->abp/dot_general | solution.py:24
  269.1 0.0 reduce-scatter.5.cloned.1.call-update
  269.2 0.0 reduce-scatter.7.cloned.1.call-start
  269.2 96.1 %reduce-scatter.5.cloned.1.call-done = f32[2,32,1024]{2,1,0:T(8,128)} async-done(((f32[32,32,1024]{2,1,0:T(8,128)}), f32[2,32,1024]{2,1,0:T(8,128)}) %reduce-scatter.5.cloned.1.call-update) | async-done | bytes 262160 | tf_op jit(solution)/shard_map/reduce_scatter | solution.py:23
  365.4 1.4 copy.52
  366.8 1.4 reshape.21
  368.2 0.0 reduce-scatter.7.cloned.1.call-update
  368.2 74.4 %reduce-scatter.7.cloned.1.call-done = f32[64,64]{1,0:T(8,128)} async-done(((f32[1024,64]{1,0:T(8,128)}), f32[64,64]{1,0:T(8,128)}) %reduce-scatter.7.cloned.1.call-update) | async-done | bytes 16400
  442.6 0.8 reshape.22
  443.4 0.1 copy.53
  443.5 0.1 reshape.16
  443.6 0.1 copy.42
  443.7 0.1 reshape.25
  443.8 13.9 %all_to_all.43 = bf16[16,2,128]{2,1,0:T(2,128)(2,1)S(1)} all-to-all(bf16[16,2,128]{2,1,0:T(2,128)(2,1)S(1)} %reshape.25), channel_id=1, replica_groups=mesh['row'=16,'col'=16] {'row'}, dimensions={0} | all-to-all | bytes 16384 | tf_op jit(solution)/shard_map/all_to_all | solution.py:33
  457.7 0.1 reshape.26
  457.8 0.1 copy.45
  457.9 0.1 reshape.27
  458.0 14.0 %all_to_all.44 = bf16[16,2,128]{2,1,0:T(2,128)(2,1)S(1)} all-to-all(bf16[16,2,128]{2,1,0:T(2,128)(2,1)S(1)} %reshape.27), channel_id=1, replica_groups=mesh['row'=16,'col'=16] {'col'}, dimensions={0} | all-to-all | bytes 16384 | tf_op jit(solution)/shard_map/all_to_all | solution.py:32
  472.0 0.1 reshape.28
  472.2 0.1 copy.47
  472.2 0.7 fusion.3
  (5 shorter events, 0.1 us)
Async XLA Ops:
  6.5 358.8 %reduce-scatter.5.cloned.1.call-start = ((), (), s32[]{:S(2)}) async-start(), calls=%async_computation.5 | async-start | bytes 4456448 | tf_op jit(solution)/shard_map/reduce_scatter | solution.py:23
  223.5 36.0 %slice-start = ((s8[6422528]{0:T(1024)(128)(4,1)}), s8[2228224]{0:T(1024)(128)(4,1)S(1)}, s32[]{:S(2)}) async-start(s8[6422528]{0:T(1024)(128)(4,1)} %bitcast.54), calls=%async_computation.7 | async-start | bytes 4456448
  250.3 9.1 %slice-start.1 = ((s8[6422528]{0:T(1024)(128)(4,1)}), s8[4194304]{0:T(1024)(128)(4,1)S(1)}, s32[]{:S(2)}) async-start(s8[6422528]{0:T(1024)(128)(4,1)} %bitcast.54), calls=%async_computation.8 | async-start | bytes 8388608
  269.2 173.4 %reduce-scatter.7.cloned.1.call-start = ((), (), s32[]{:S(2)}) async-start(), calls=%async_computation.6 | async-start | bytes 557056
Sparse Core Ops, SparseCore 0:
  269.3 96.0 reduce-scatter.4
  369.4 73.0 reduce-scatter.6
where the time goes:
time: 481 us; the launch traced here: 480 us
  blocking collectives  181 us (38%)
  waiting for transfers between devices  171 us (36%)
  local copies, waits for them, and re-layouts  104 us (22%)
  between operations  13.5 us (3%)
  matrix products  9.65 us (2%)
    all_to_all x1, blocking collectives, shards(): lax.all_to_all(integrals, 'col', split_axis=2, concat_axis=1, tiled=True)  153 us
    reduce_scatter x1, waiting for transfers between devices, shards(): lax.psum_scatter(jnp.einsum('cadb,cdp->abp', weights, amp_block, preferre...  96.1 us
    unnamed x15, local copies, waits for them, and re-layouts  94.5 us
    unnamed x3, waiting for transfers between devices  74.4 us
    all_to_all x1, blocking collectives, shards(): lax.all_to_all(lax.all_to_all(ladder, 'row', split_axis=3, concat_axis=2,...  14 us
    all_to_all x1, blocking collectives, shards(): lax.all_to_all(ladder, 'row', split_axis=3, concat_axis=2, tiled=True)  13.9 us
    dot_general x1, matrix products, shards(): jnp.einsum('cadb,cdp->abp', weights, amp_block, preferred_element_type=jn...  9.65 us
  transfers between devices with their start and end apart: 2, of which 2 were waited for; matrix products, arithmetic and copies ran while one was open for 0% of the time, Pallas kernels for 0%

commit v1 on v0

v1 whole, which is shorter than its diff:
```python
import jax
import jax.numpy as jnp
from jax import lax
from jax.experimental import pallas as pl
from jax.experimental.pallas import tpu as pltpu
from jax.sharding import PartitionSpec as P

MESH = pl.DeviceIdType.MESH
F32 = jnp.float32
BF16 = jnp.bfloat16

ROWS = 16
COLS = 16
CW = 56
DW = 56
VB = 32
OB = 32
PAIRS = OB * OB
GROUPS = 8
PIECES = 7
LANES = DW * VB // PIECES
TILES = LANES // 128
KP = TILES * 256


def kernel(w_ref, t_ref, o_ref, wbuf, tbuf, lhs, rhs, acc, folded, row_out, row_in, direct, mirror,
           col_out, col_in, w_send, w_recv, t_sem, row_send, row_recv, col_send, col_recv):
    r = lax.axis_index("row")
    q = lax.axis_index("col")
    z, y = q // 2, q % 2

    def step(g, h):
        far = (g // 2 + 3) // 4
        dz = (1 - far) * 4 * (g % 2) + far * (4 - g // 2) * (1 - 2 * h)
        dy = (1 - far) * h + far * (g % 2)
        return dz, dy

    def target(g, h):
        dz, dy = step(g, h)
        return lax.rem(z + dz + 8, 8) * 2 + lax.rem(y + dy, 2)

    def origin(g, h):
        dz, dy = step(g, h)
        return lax.rem(z - dz + 8, 8) * 2 + lax.rem(y - dy + 2, 2)

    def piece(g, h, k):
        return wbuf.at[g * 2 + h, :, :, pl.ds(pl.multiple_of(k * LANES, 128), LANES)]

    def send_piece(g, h, k):
        p = target(g, h)
        columns = pl.ds(pl.multiple_of(p * (DW * VB) + k * LANES, 128), LANES)
        return pltpu.make_async_remote_copy(
            src_ref=w_ref.at[:, :, columns], dst_ref=piece(g, h, k),
            send_sem=w_send.at[g, h], recv_sem=w_recv.at[g, h, k],
            device_id=(r, p), device_id_type=MESH)

    def local_copy(k):
        columns = pl.ds(pl.multiple_of(q * (DW * VB) + k * LANES, 128), LANES)
        return pltpu.make_async_copy(w_ref.at[:, :, columns], piece(0, 0, k), w_recv.at[0, 0, k])

    t_copy = pltpu.make_async_copy(t_ref, tbuf, t_sem)
    t_copy.start()

    barrier = pltpu.get_barrier_semaphore()
    for k in range(1, COLS):
        pl.semaphore_signal(barrier, inc=1, device_id=(r, lax.rem(q + k, COLS)), device_id_type=MESH)
    for k in range(1, ROWS):
        pl.semaphore_signal(barrier, inc=1, device_id=(lax.rem(r + k, ROWS), q), device_id_type=MESH)
    pl.semaphore_wait(barrier, COLS + ROWS - 2)

    @pl.loop(0, PIECES)
    def _(k):
        local_copy(k).start()
        send_piece(0, 1, k).start()

    @pl.loop(1, GROUPS)
    def _(g):
        @pl.loop(0, PIECES)
        def _(k):
            send_piece(g, 0, k).start()
            send_piece(g, 1, k).start()

    t_copy.wait()
    gap = jnp.zeros((8, PAIRS), F32)

    @pl.loop(0, PIECES)
    def _(k):
        for n in range(KP // 128):
            base = pl.multiple_of((k * (KP // 128) + n) * 2 * PAIRS, 128)
            first = tbuf[:, pl.ds(base, PAIRS)].astype(F32)
            second = tbuf[:, pl.ds(base + PAIRS, PAIRS)].astype(F32)
            both = jnp.concatenate([first, gap, second, gap], axis=0)
            lhs[k, :, n * 128:(n + 1) * 128] = both.T.astype(BF16)

    lane = lax.broadcasted_iota(jnp.int32, (64, 128), 1)
    pad = jnp.zeros((8, 128), F32)

    def compute(g):
        acc[...] = jnp.zeros_like(acc)

        @pl.loop(0, PIECES)
        def _(k):
            for h in range(2):
                pltpu.make_async_copy(piece(g, h, k), piece(g, h, k), w_recv.at[g, h, k]).wait()
            for h in range(2):
                for t in range(TILES):
                    columns = pl.ds(pl.multiple_of(k * LANES + t * 128, 128), 128)
                    x = wbuf[g * 2 + h, :, :, columns].astype(F32)
                    for a in range(2):
                        xa = jnp.concatenate([x[:, a, :], pad], axis=0)
                        for d in range(4):
                            rhs[t * 256 + d * 64:t * 256 + (d + 1) * 64,
                                h * 256 + a * 128:h * 256 + (a + 1) * 128] = (
                                jnp.where(lane // 32 == d, xa, 0.0).astype(BF16))
            acc[...] += jnp.dot(lhs[k], rhs[...], preferred_element_type=F32)

    low = lax.broadcasted_iota(jnp.int32, (32, 128), 1) < 64
    even = lane // 32 % 2 == 0

    def fold(x):
        x = x + pltpu.roll(x, 64, 1)
        return x + pltpu.roll(x, 32, 1)

    def scatter(g):
        for h in range(2):
            @pl.loop(0, ROWS)
            def _(p):
                rows = pl.ds(pl.multiple_of(p * 64, 64), 64)
                x = jnp.where(even, fold(acc[rows, h * 256:h * 256 + 128]),
                              fold(acc[rows, h * 256 + 128:h * 256 + 256]))
                folded[rows, :] = x
                row_out[g, p, h, 0] = jnp.where(low, x[:32], x[32:]).astype(BF16)

            @pl.loop(0, ROWS)
            def _(p):
                x0 = folded[pl.ds(2 * p, 32, stride=32), :]
                x1 = folded[pl.ds(2 * p + 1, 32, stride=32), :]
                row_out[g, p, h, 1] = jnp.where(low, x0, x1).astype(BF16)

        @pl.loop(1, ROWS)
        def _(k):
            p = lax.rem(r + k, ROWS)
            pltpu.make_async_remote_copy(
                src_ref=row_out.at[g, p], dst_ref=row_in.at[g, k - 1],
                send_sem=row_send.at[g], recv_sem=row_recv.at[g],
                device_id=(p, q), device_id_type=MESH).start()

    quarter = lax.broadcasted_iota(jnp.int32, (32, 128), 1) // 32

    def collect(g):
        pltpu.make_async_copy(row_in.at[g], row_in.at[g], row_recv.at[g]).wait()
        sums = [row_out[g, r, h, m].astype(F32) for h in range(2) for m in range(2)]
        for k in range(ROWS - 1):
            for h in range(2):
                for m in range(2):
                    sums[h * 2 + m] += row_in[g, k, h, m].astype(F32)
        turned = jnp.concatenate(sums, axis=0).T
        for h in range(2):
            p = origin(g, h)
            out = jnp.zeros((32, 128), F32)
            for n in range(4):
                block = turned[n * 32:(n + 1) * 32]
                shift = (n * 32 - h * 64) % 128
                moved = pltpu.roll(block, shift, 1) if shift else block
                out = jnp.where(quarter == n, moved, out)
                rows = pl.ds(pl.multiple_of((2 * p + n % 2) * 32, 32), 32)
                mirror[n // 2, rows, :] = pltpu.roll(block, (128 - h * 64 - 32) % 128, 1)
            direct[p] = out

    @pl.loop(0, GROUPS)
    def _(g):
        compute(g)
        scatter(g)

        @pl.when(g > 0)
        def _():
            collect(g - 1)

    collect(GROUPS - 1)

    def finish(p):
        out = jnp.zeros((32, 128), F32)
        for n in range(4):
            x = mirror[n // 2, pl.ds(2 * p + n % 2, 32, stride=32), :]
            out = jnp.where(quarter == n, pltpu.roll(x, n * 32, 1) if n else x, out)
        return direct[p] + out

    @pl.loop(1, COLS)
    def _(k):
        p = lax.rem(q + k, COLS)
        col_out[k - 1] = finish(p).astype(BF16)
        pltpu.make_async_remote_copy(
            src_ref=col_out.at[k - 1], dst_ref=col_in.at[k - 1],
            send_sem=col_send, recv_sem=col_recv,
            device_id=(r, p), device_id_type=MESH).start()

    total = finish(q)
    pltpu.make_async_copy(col_in, col_in, col_recv).wait()
    for k in range(COLS - 1):
        total += col_in[k].astype(F32)
    o_ref[...] = total.astype(BF16)

    pltpu.make_async_copy(col_out, col_out, col_send).wait()

    @pl.loop(0, GROUPS)
    def _(g):
        pltpu.make_async_copy(row_in.at[g], row_in.at[g], row_send.at[g]).wait()
        pltpu.make_async_copy(wbuf.at[g * 2 + 1], wbuf.at[g * 2 + 1], w_send.at[g, 1]).wait()

    @pl.loop(1, GROUPS)
    def _(g):
        pltpu.make_async_copy(wbuf.at[g * 2], wbuf.at[g * 2], w_send.at[g, 0]).wait()


def shards(integrals, amplitudes):
    out = pl.pallas_call(
        kernel,
        out_shape=jax.ShapeDtypeStruct((VB, 128), BF16),
        in_specs=[pl.BlockSpec(memory_space=pl.ANY)] * 2,
        out_specs=pl.BlockSpec(memory_space=pltpu.VMEM),
        scratch_shapes=[
            pltpu.VMEM((2 * GROUPS, CW, 2, DW * VB), BF16),
            pltpu.VMEM((CW, DW * PAIRS), BF16),
            pltpu.VMEM((PIECES, PAIRS, KP), BF16),
            pltpu.VMEM((KP, 512), BF16),
            pltpu.VMEM((PAIRS, 512), F32),
            pltpu.VMEM((PAIRS, 128), F32),
            pltpu.VMEM((GROUPS, ROWS, 2, 2, 32, 128), BF16),
            pltpu.VMEM((GROUPS, ROWS - 1, 2, 2, 32, 128), BF16),
            pltpu.VMEM((COLS, 32, 128), F32),
            pltpu.VMEM((2, PAIRS, 128), F32),
            pltpu.VMEM((COLS - 1, 32, 128), BF16),
            pltpu.VMEM((COLS - 1, 32, 128), BF16),
            pltpu.SemaphoreType.DMA((GROUPS, 2)),
            pltpu.SemaphoreType.DMA((GROUPS, 2, PIECES)),
            pltpu.SemaphoreType.DMA,
            pltpu.SemaphoreType.DMA((GROUPS,)),
            pltpu.SemaphoreType.DMA((GROUPS,)),
            pltpu.SemaphoreType.DMA,
            pltpu.SemaphoreType.DMA,
        ],
        compiler_params=pltpu.CompilerParams(
            collective_id=0, has_side_effects=True, vmem_limit_bytes=56 * 2**20),
        cost_estimate=pl.CostEstimate(flops=26 * 10**9, bytes_accessed=13 * 10**6, transcendentals=0),
    )(integrals, amplitudes)
    return jnp.transpose(out.reshape(VB, 2, 2, OB), (2, 0, 1, 3))


def solution(mesh):
    return jax.shard_map(
        shards,
        mesh=mesh,
        in_specs=(P("row", "col", None), P("row", "col")),
        out_specs=P("col", None, "row", None),
        check_vma=False,
    )
```

time: 481 us -> 220 us (0.46)
  Pallas kernels: 0 us -> 219 us
  blocking collectives: 181 us -> 0 us
  waiting for transfers between devices: 171 us -> 0 us
  local copies, waits for them, and re-layouts: 104 us -> 1.42 us
  between operations: 13.5 us -> 0.01 us
  matrix products: 9.65 us -> 0 us
    pallas_call x0 -> x1, Pallas kernels: none -> 219 us  [shards(): pl.pallas_call(kernel, out_shape=jax.ShapeDtypeStruct((VB, 128), BF16), i...]
    all_to_all x3 -> x0, blocking collectives: 181 us -> none  [the longest x1 153 us: shards(): lax.all_to_all(integrals, 'col', split_axis=2, concat_axis=1, tiled=True)]
    reduce_scatter x1 -> x0, waiting for transfers between devices: 96.1 us -> none  [shards(): lax.psum_scatter(jnp.einsum('cadb,cdp->abp', weights, amp_block, preferre...]
    unnamed x15 -> x0, local copies, waits for them, and re-layouts: 94.5 us -> none
    unnamed x3 -> x0, waiting for transfers between devices: 74.4 us -> none
    dot_general x1 -> x0, matrix products: 9.65 us -> none  [shards(): jnp.einsum('cadb,cdp->abp', weights, amp_block, preferred_element_type=jn...]
    all_to_all x5 -> x0, local copies, waits for them, and re-layouts: 9.26 us -> none  [the longest x1 9.12 us: shards(): lax.all_to_all(integrals, 'col', split_axis=2, concat_axis=1, tiled=True)]
  transfers between devices with their start and end apart: 2 -> 0, of which waited for: 2 -> 0; matrix products, arithmetic and copies ran while one was open for 0% -> 0% of each run, Pallas kernels for 0% -> 0%
where the time goes in v1:
time: 220 us
  Pallas kernels  219 us (100%)
    pallas_call x1, Pallas kernels, shards(): pl.pallas_call(kernel, out_shape=jax.ShapeDtypeStruct((VB, 128), BF16), i...  219 us

profile of v1, /device:TPU:1, one launch (start us, length us, event | category | flops | bytes accessed | tf_op | source)
XLA Modules:
  0.0 220.1 jit_solution(752085994993207397)
XLA Ops:
  0.0 218.6 %shard_map.28 = bf16[32,128]{1,0:T(8,128)(2,1)} custom-call(bf16[56,2,28672]{2,1,0:T(2,128)(2,1)} %w_ref.1, bf16[56,57344]{1,0:T(8,128)(2,1)} %t_ref.1), custom_call_target="tpu_custom_call" | custom-call | flops 25999998976 | bytes 13000000 | tf_op jit(solution)/shard_map/pallas_call | solution.py:216
  218.6 0.8 reshape.3
  219.4 0.6 copy.5

commit v2 on v1

v2 whole, which is shorter than its diff:
```python
import jax
import jax.numpy as jnp
from jax import lax
from jax.experimental import pallas as pl
from jax.experimental.pallas import tpu as pltpu
from jax.sharding import PartitionSpec as P

MESH = pl.DeviceIdType.MESH
F32 = jnp.float32
BF16 = jnp.bfloat16

ROWS = 16
CHIPS = 8
COLS = 16
CW = 56
DW = 56
VB = 32
OB = 32
PAIRS = OB * OB
GROUPS = 8
PIECES = 7
LANES = DW * VB // PIECES
TILES = LANES // 128
KP = TILES * 256


def kernel(w_ref, t_ref, o_ref, wbuf, tbuf, lhs, rhs, acc, cross, core_in, row_out, row_in, direct, mirror,
           col_out, col_in, w_send, w_recv, t_sem, core_send, core_recv, row_send, row_recv, col_send, col_recv):
    r = lax.axis_index("row")
    q = lax.axis_index("col")
    z, y = q // 2, q % 2
    u, c = r // 2, r % 2

    def step(g, h):
        i = g % 4
        far = (i + 3) // 4
        dz = (1 - far) * 4 * (1 - h) + far * (4 - i) * (1 - 2 * h)
        return dz, 1 - g // 4

    def target(g, h):
        dz, dy = step(g, h)
        return lax.rem(z + dz + 8, 8) * 2 + lax.rem(y + dy, 2)

    def origin(g, h):
        dz, dy = step(g, h)
        return lax.rem(z - dz + 8, 8) * 2 + lax.rem(y - dy + 2, 2)

    def piece(g, h, k):
        return wbuf.at[g * 2 + h, :, :, pl.ds(pl.multiple_of(k * LANES, 128), LANES)]

    def send_piece(g, h, k):
        p = target(g, h)
        columns = pl.ds(pl.multiple_of(p * (DW * VB) + k * LANES, 128), LANES)
        return pltpu.make_async_remote_copy(
            src_ref=w_ref.at[:, :, columns], dst_ref=piece(g, h, k),
            send_sem=w_send.at[g, h], recv_sem=w_recv.at[g, h, k],
            device_id=(r, p), device_id_type=MESH)

    def local_copy(k):
        columns = pl.ds(pl.multiple_of(q * (DW * VB) + k * LANES, 128), LANES)
        return pltpu.make_async_copy(w_ref.at[:, :, columns], piece(4, 1, k), w_recv.at[4, 1, k])

    t_copy = pltpu.make_async_copy(t_ref, tbuf, t_sem)
    t_copy.start()

    barrier = pltpu.get_barrier_semaphore()
    for k in range(1, COLS):
        pl.semaphore_signal(barrier, inc=1, device_id=(r, lax.rem(q + k, COLS)), device_id_type=MESH)
    for k in range(1, ROWS):
        pl.semaphore_signal(barrier, inc=1, device_id=(lax.rem(r + k, ROWS), q), device_id_type=MESH)
    pl.semaphore_wait(barrier, COLS + ROWS - 2)

    for slot in range(2 * GROUPS + PIECES - 2):
        @pl.loop(max(0, slot - PIECES + 2) // 2, min(GROUPS - 1, slot // 2) + 1)
        def _(g):
            send_piece(g, 0, slot - 2 * g).start()

            @pl.when(g != 4)
            def _():
                send_piece(g, 1, slot - 2 * g).start()

    @pl.loop(0, PIECES)
    def _(k):
        local_copy(k).start()

    t_copy.wait()
    gap = jnp.zeros((8, PAIRS), F32)

    @pl.loop(0, PIECES)
    def _(k):
        for n in range(KP // 128):
            base = pl.multiple_of((k * (KP // 128) + n) * 2 * PAIRS, 128)
            first = tbuf[:, pl.ds(base, PAIRS)].astype(F32)
            second = tbuf[:, pl.ds(base + PAIRS, PAIRS)].astype(F32)
            both = jnp.concatenate([first, gap, second, gap], axis=0)
            lhs[k, :, n * 128:(n + 1) * 128] = both.T.astype(BF16)

    @pl.loop(0, GROUPS)
    def _(g):
        acc[g] = jnp.zeros((PAIRS, 128), F32)

    quarter = lax.broadcasted_iota(jnp.int32, (CW, 128), 1) // 32
    pad = jnp.zeros((8, 128), F32)

    def compute(g, k):
        for h in range(2):
            pltpu.make_async_copy(piece(g, h, k), piece(g, h, k), w_recv.at[g, h, k]).wait()
        for t in range(TILES):
            columns = pl.ds(pl.multiple_of(k * LANES + t * 128, 128), 128)
            x = [wbuf[g * 2 + h, :, :, columns].astype(F32) for h in range(2)]
            x = [x[h][:, a, :] for h in range(2) for a in range(2)]
            for d in range(4):
                out = None
                for n in range(4):
                    moved = pltpu.roll(x[n], (n - d) % 4 * 32, 1) if n != d else x[n]
                    out = jnp.where(quarter == n, moved, out) if n else moved
                rhs[t * 256 + d * 64:t * 256 + (d + 1) * 64] = (
                    jnp.concatenate([out, pad], axis=0).astype(BF16))
        acc[g] += jnp.dot(lhs[k], rhs[...], preferred_element_type=F32)

    def cross_copy(g):
        return pltpu.make_async_remote_copy(
            src_ref=cross.at[g, 1 - c], dst_ref=core_in.at[g, 1],
            send_sem=core_send.at[g, 1], recv_sem=core_recv.at[g, 1],
            device_id=(r + 1 - 2 * c, q), device_id_type=MESH)

    def mine(p, core):
        return pl.ds(pl.multiple_of((p * 2 + core) * 64, 64), 64)

    def scatter(g):
        @pl.loop(0, CHIPS)
        def _(p):
            pltpu.make_async_remote_copy(
                src_ref=acc.at[g, mine(p, 1 - c)], dst_ref=core_in.at[g, 0, p],
                send_sem=core_send.at[g, 0], recv_sem=core_recv.at[g, 0],
                device_id=(r + 1 - 2 * c, q), device_id_type=MESH).start()

        for j in range(OB):
            cross[g, j // 2 % 2, j // 4, j % 2 * 32:(j % 2 + 1) * 32] = acc[g, pl.ds(j, 32, stride=32), :]
        cross_copy(g).start()

    def pair(g):
        pltpu.make_async_copy(core_in.at[g, 0], core_in.at[g, 0], core_recv.at[g, 0]).wait()
        cross_copy(g).wait_recv()

        @pl.loop(1, CHIPS)
        def _(k):
            p = lax.rem(u + k, CHIPS)
            row_out[g, p, 0] = (acc[g, mine(p, c)] + core_in[g, 0, p]).astype(BF16)
            row_out[g, p, 1] = (cross[g, c, p] + core_in[g, 1, p]).astype(BF16)
            pltpu.make_async_remote_copy(
                src_ref=row_out.at[g, p], dst_ref=row_in.at[g, k - 1],
                send_sem=row_send.at[g], recv_sem=row_recv.at[g],
                device_id=(p * 2 + c, q), device_id_type=MESH).start()

    low = lax.broadcasted_iota(jnp.int32, (32, 128), 1) < 64

    def collect(g):
        straight = acc[g, mine(u, c)] + core_in[g, 0, u]
        crossed = cross[g, c, u] + core_in[g, 1, u]
        pltpu.make_async_copy(row_in.at[g], row_in.at[g], row_recv.at[g]).wait()
        for k in range(CHIPS - 1):
            straight += row_in[g, k, 0].astype(F32)
            crossed += row_in[g, k, 1].astype(F32)
        turned = jnp.concatenate([straight, crossed], axis=0).T
        for h in range(2):
            p = origin(g, h)
            x0 = turned[h * 64:h * 64 + 32]
            x1 = turned[h * 64 + 32:h * 64 + 64]
            direct[p] = jnp.where(low, x0, pltpu.roll(x1, 64, 1))
            mirror[pl.ds(pl.multiple_of(p * 64, 64), 64), :] = turned[h * 64:h * 64 + 64]

    @pl.loop(0, GROUPS)
    def _(g):
        @pl.loop(0, PIECES)
        def _(k):
            compute(g, k)

            @pl.when((k == 1) & (g > 0))
            def _():
                pair(g - 1)

            @pl.when((k == 4) & (g > 0))
            def _():
                collect(g - 1)

        scatter(g)

    pair(GROUPS - 1)
    collect(GROUPS - 1)

    def finish(p):
        x0 = mirror[pl.ds(2 * p, 32, stride=32), :]
        x1 = mirror[pl.ds(2 * p + 1, 32, stride=32), :]
        return direct[p] + jnp.where(low, pltpu.roll(x0, 64, 1), x1)

    @pl.loop(1, COLS, unroll=5)
    def _(k):
        p = lax.rem(q + k, COLS)
        col_out[k - 1] = finish(p).astype(BF16)
        pltpu.make_async_remote_copy(
            src_ref=col_out.at[k - 1], dst_ref=col_in.at[k - 1],
            send_sem=col_send, recv_sem=col_recv,
            device_id=(r, p), device_id_type=MESH).start()

    total = finish(q)
    pltpu.make_async_copy(col_in, col_in, col_recv).wait()
    for k in range(COLS - 1):
        total += col_in[k].astype(F32)
    o_ref[...] = total.astype(BF16)

    pltpu.make_async_copy(col_out, col_out, col_send).wait()

    @pl.loop(0, GROUPS)
    def _(g):
        pltpu.make_async_copy(core_in.at[g, 0], core_in.at[g, 0], core_send.at[g, 0]).wait()
        cross_copy(g).wait_send()
        pltpu.make_async_copy(row_in.at[g], row_in.at[g], row_send.at[g]).wait()
        pltpu.make_async_copy(wbuf.at[g * 2], wbuf.at[g * 2], w_send.at[g, 0]).wait()

        @pl.when(g != 4)
        def _():
            pltpu.make_async_copy(wbuf.at[g * 2 + 1], wbuf.at[g * 2 + 1], w_send.at[g, 1]).wait()


def shards(integrals, amplitudes):
    out = pl.pallas_call(
        kernel,
        out_shape=jax.ShapeDtypeStruct((VB, 128), BF16),
        in_specs=[pl.BlockSpec(memory_space=pl.ANY)] * 2,
        out_specs=pl.BlockSpec(memory_space=pltpu.VMEM),
        scratch_shapes=[
            pltpu.VMEM((2 * GROUPS, CW, 2, DW * VB), BF16),
            pltpu.VMEM((CW, DW * PAIRS), BF16),
            pltpu.VMEM((PIECES, PAIRS, KP), BF16),
            pltpu.VMEM((KP, 128), BF16),
            pltpu.VMEM((GROUPS, PAIRS, 128), F32),
            pltpu.VMEM((GROUPS, 2, CHIPS, 64, 128), F32),
            pltpu.VMEM((GROUPS, 2, CHIPS, 64, 128), F32),
            pltpu.VMEM((GROUPS, CHIPS, 2, 64, 128), BF16),
            pltpu.VMEM((GROUPS, CHIPS - 1, 2, 64, 128), BF16),
            pltpu.VMEM((COLS, 32, 128), F32),
            pltpu.VMEM((PAIRS, 128), F32),
            pltpu.VMEM((COLS - 1, 32, 128), BF16),
            pltpu.VMEM((COLS - 1, 32, 128), BF16),
            pltpu.SemaphoreType.DMA((GROUPS, 2)),
            pltpu.SemaphoreType.DMA((GROUPS, 2, PIECES)),
            pltpu.SemaphoreType.DMA,
            pltpu.SemaphoreType.DMA((GROUPS, 2)),
            pltpu.SemaphoreType.DMA((GROUPS, 2)),
            pltpu.SemaphoreType.DMA((GROUPS,)),
            pltpu.SemaphoreType.DMA((GROUPS,)),
            pltpu.SemaphoreType.DMA,
            pltpu.SemaphoreType.DMA,
        ],
        compiler_params=pltpu.CompilerParams(
            collective_id=0, has_side_effects=True, vmem_limit_bytes=56 * 2**20),
        cost_estimate=pl.CostEstimate(flops=13 * 10**9, bytes_accessed=13 * 10**6, transcendentals=0),
    )(integrals, amplitudes)
    return jnp.transpose(out.reshape(VB, 2, 2, OB), (1, 0, 2, 3))


def solution(mesh):
    return jax.shard_map(
        shards,
        mesh=mesh,
        in_specs=(P("row", "col", None), P("row", "col")),
        out_specs=P("col", None, "row", None),
        check_vma=False,
    )
```

time: 220 us -> 184 us (0.84)
  Pallas kernels: 219 us -> 182 us
    pallas_call x1, Pallas kernels: 219 us -> 182 us  [shards(): pl.pallas_call(kernel, out_shape=jax.ShapeDtypeStruct((VB, 128), BF16), i...]
where the time goes in v2:
time: 184 us
  Pallas kernels  182 us (99%)
    pallas_call x1, Pallas kernels, shards(): pl.pallas_call(kernel, out_shape=jax.ShapeDtypeStruct((VB, 128), BF16), i...  182 us

profile of v2, /device:TPU:1, one launch (start us, length us, event | category | flops | bytes accessed | tf_op | source)
XLA Modules:
  0.0 183.6 jit_solution(1937791566630763300)
XLA Ops:
  0.0 182.2 %shard_map.28 = bf16[32,128]{1,0:T(8,128)(2,1)} custom-call(bf16[56,2,28672]{2,1,0:T(2,128)(2,1)} %w_ref.1, bf16[56,57344]{1,0:T(8,128)(2,1)} %t_ref.1), custom_call_target="tpu_custom_call" | custom-call | flops 12999999488 | bytes 13000000 | tf_op jit(solution)/shard_map/pallas_call | solution.py:227
  182.2 0.8 reshape.3
  182.9 0.6 copy.5

commit v3 on v2

--- a/solution.py
+++ b/solution.py
@@ -24,8 +24,8 @@
 KP = TILES * 256
 
 
-def kernel(w_ref, t_ref, o_ref, wbuf, tbuf, lhs, rhs, acc, cross, core_in, row_out, row_in, direct, mirror,
-           col_out, col_in, w_send, w_recv, t_sem, core_send, core_recv, row_send, row_recv, col_send, col_recv):
+def kernel(w_ref, t_ref, o_ref, wbuf, tbuf, lhs, rhs, acc, core_in, row_out, row_in, own, swap_out, swap_in, turn, crossed, direct, mirror,
+           col_out, col_in, w_send, w_recv, t_sem, core_send, core_recv, row_send, row_recv, swap_send, swap_recv, col_send, col_recv):
     r = lax.axis_index("row")
     q = lax.axis_index("col")
     z, y = q // 2, q % 2
@@ -98,6 +98,7 @@
     @pl.loop(0, GROUPS)
     def _(g):
         acc[g] = jnp.zeros((PAIRS, 128), F32)
+        swap_out[g] = jnp.zeros((ROWS, 8, 128), F32)
 
     quarter = lax.broadcasted_iota(jnp.int32, (CW, 128), 1) // 32
     pad = jnp.zeros((8, 128), F32)
@@ -118,51 +119,59 @@
                     jnp.concatenate([out, pad], axis=0).astype(BF16))
         acc[g] += jnp.dot(lhs[k], rhs[...], preferred_element_type=F32)
 
-    def cross_copy(g):
-        return pltpu.make_async_remote_copy(
-            src_ref=cross.at[g, 1 - c], dst_ref=core_in.at[g, 1],
-            send_sem=core_send.at[g, 1], recv_sem=core_recv.at[g, 1],
-            device_id=(r + 1 - 2 * c, q), device_id_type=MESH)
-
     def mine(p, core):
         return pl.ds(pl.multiple_of((p * 2 + core) * 64, 64), 64)
 
     def scatter(g):
-        @pl.loop(0, CHIPS)
+        @pl.loop(0, CHIPS, unroll=True)
         def _(p):
             pltpu.make_async_remote_copy(
-                src_ref=acc.at[g, mine(p, 1 - c)], dst_ref=core_in.at[g, 0, p],
-                send_sem=core_send.at[g, 0], recv_sem=core_recv.at[g, 0],
+                src_ref=acc.at[g, mine(p, 1 - c)], dst_ref=core_in.at[g, p],
+                send_sem=core_send.at[g], recv_sem=core_recv.at[g],
                 device_id=(r + 1 - 2 * c, q), device_id_type=MESH).start()
 
-        for j in range(OB):
-            cross[g, j // 2 % 2, j // 4, j % 2 * 32:(j % 2 + 1) * 32] = acc[g, pl.ds(j, 32, stride=32), :]
-        cross_copy(g).start()
-
     def pair(g):
-        pltpu.make_async_copy(core_in.at[g, 0], core_in.at[g, 0], core_recv.at[g, 0]).wait()
-        cross_copy(g).wait_recv()
-
-        @pl.loop(1, CHIPS)
+        pltpu.make_async_copy(core_in.at[g], core_in.at[g], core_recv.at[g]).wait()
+
+        @pl.loop(1, CHIPS, unroll=True)
         def _(k):
             p = lax.rem(u + k, CHIPS)
-            row_out[g, p, 0] = (acc[g, mine(p, c)] + core_in[g, 0, p]).astype(BF16)
-            row_out[g, p, 1] = (cross[g, c, p] + core_in[g, 1, p]).astype(BF16)
+            row_out[g, p] = (acc[g, mine(p, c)] + core_in[g, p]).astype(BF16)
             pltpu.make_async_remote_copy(
                 src_ref=row_out.at[g, p], dst_ref=row_in.at[g, k - 1],
                 send_sem=row_send.at[g], recv_sem=row_recv.at[g],
                 device_id=(p * 2 + c, q), device_id_type=MESH).start()
 
-    low = lax.broadcasted_iota(jnp.int32, (32, 128), 1) < 64
-
-    def collect(g):
-        straight = acc[g, mine(u, c)] + core_in[g, 0, u]
-        crossed = cross[g, c, u] + core_in[g, 1, u]
+    def column(g):
+        straight = acc[g, mine(u, c)] + core_in[g, u]
         pltpu.make_async_copy(row_in.at[g], row_in.at[g], row_recv.at[g]).wait()
         for k in range(CHIPS - 1):
-            straight += row_in[g, k, 0].astype(F32)
-            crossed += row_in[g, k, 1].astype(F32)
-        turned = jnp.concatenate([straight, crossed], axis=0).T
+            straight += row_in[g, k].astype(F32)
+        own[g] = straight
+        for p in range(ROWS):
+            swap_out[g, p, 0:2] = straight[2 * p:2 * p + 2]
+            swap_out[g, p, 2:4] = straight[OB + 2 * p:OB + 2 * p + 2]
+
+        @pl.loop(1, ROWS, unroll=5)
+        def _(k):
+            p = lax.rem(r + k, ROWS)
+            pltpu.make_async_remote_copy(
+                src_ref=swap_out.at[g, p], dst_ref=swap_in.at[g, r],
+                send_sem=swap_send.at[g], recv_sem=swap_recv.at[g],
+                device_id=(p, q), device_id_type=MESH).start()
+
+        swap_in[g, r] = swap_out[g, r]
+
+    low = lax.broadcasted_iota(jnp.int32, (32, 128), 1) < 64
+
+    def collect(g):
+        pltpu.make_async_copy(swap_in.at[g, 1:ROWS], swap_in.at[g, 1:ROWS], swap_recv.at[g]).wait()
+        flat = swap_in[g].reshape(ROWS * 8, 128)
+        turn[...] = flat
+        for j in range(2):
+            for i in range(2):
+                crossed[pl.ds(j * OB + i, ROWS, stride=2), :] = turn[pl.ds(2 * i + j, ROWS, stride=8), :]
+        turned = jnp.concatenate([own[g], crossed[...]], axis=0).T
         for h in range(2):
             p = origin(g, h)
             x0 = turned[h * 64:h * 64 + 32]
@@ -176,17 +185,26 @@
         def _(k):
             compute(g, k)
 
-            @pl.when((k == 1) & (g > 0))
-            def _():
-                pair(g - 1)
-
-            @pl.when((k == 4) & (g > 0))
-            def _():
-                collect(g - 1)
+            early = 2 * (g - GROUPS // 2)
+            for n in range(2):
+                late = (g >= GROUPS // 2) & (early + n < GROUPS - 1)
+
+                @pl.when((k == n) & late)
+                def _():
+                    pair(early + n)
+
+                @pl.when((k == 2 + n) & late)
+                def _():
+                    column(early + n)
+
+                @pl.when((k == 4 + n) & late)
+                def _():
+                    collect(early + n)
 
         scatter(g)
 
     pair(GROUPS - 1)
+    column(GROUPS - 1)
     collect(GROUPS - 1)
 
     def finish(p):
@@ -213,8 +231,8 @@
 
     @pl.loop(0, GROUPS)
     def _(g):
-        pltpu.make_async_copy(core_in.at[g, 0], core_in.at[g, 0], core_send.at[g, 0]).wait()
-        cross_copy(g).wait_send()
+        pltpu.make_async_copy(core_in.at[g], core_in.at[g], core_send.at[g]).wait()
+        pltpu.make_async_copy(swap_in.at[g, 1:ROWS], swap_in.at[g, 1:ROWS], swap_send.at[g]).wait()
         pltpu.make_async_copy(row_in.at[g], row_in.at[g], row_send.at[g]).wait()
         pltpu.make_async_copy(wbuf.at[g * 2], wbuf.at[g * 2], w_send.at[g, 0]).wait()
 
@@ -235,10 +253,14 @@
             pltpu.VMEM((PIECES, PAIRS, KP), BF16),
             pltpu.VMEM((KP, 128), BF16),
             pltpu.VMEM((GROUPS, PAIRS, 128), F32),
-            pltpu.VMEM((GROUPS, 2, CHIPS, 64, 128), F32),
-            pltpu.VMEM((GROUPS, 2, CHIPS, 64, 128), F32),
-            pltpu.VMEM((GROUPS, CHIPS, 2, 64, 128), BF16),
-            pltpu.VMEM((GROUPS, CHIPS - 1, 2, 64, 128), BF16),
+            pltpu.VMEM((GROUPS, CHIPS, 64, 128), F32),
+            pltpu.VMEM((GROUPS, CHIPS, 64, 128), BF16),
+            pltpu.VMEM((GROUPS, CHIPS - 1, 64, 128), BF16),
+            pltpu.VMEM((GROUPS, 64, 128), F32),
+            pltpu.VMEM((GROUPS, ROWS, 8, 128), F32),
+            pltpu.VMEM((GROUPS, ROWS, 8, 128), F32),
+            pltpu.VMEM((ROWS * 8, 128), F32),
+            pltpu.VMEM((64, 128), F32),
             pltpu.VMEM((COLS, 32, 128), F32),
             pltpu.VMEM((PAIRS, 128), F32),
             pltpu.VMEM((COLS - 1, 32, 128), BF16),
@@ -246,8 +268,10 @@
             pltpu.SemaphoreType.DMA((GROUPS, 2)),
             pltpu.SemaphoreType.DMA((GROUPS, 2, PIECES)),
             pltpu.SemaphoreType.DMA,
-            pltpu.SemaphoreType.DMA((GROUPS, 2)),
-            pltpu.SemaphoreType.DMA((GROUPS, 2)),
+            pltpu.SemaphoreType.DMA((GROUPS,)),
+            pltpu.SemaphoreType.DMA((GROUPS,)),
+            pltpu.SemaphoreType.DMA((GROUPS,)),
+            pltpu.SemaphoreType.DMA((GROUPS,)),
             pltpu.SemaphoreType.DMA((GROUPS,)),
             pltpu.SemaphoreType.DMA((GROUPS,)),
             pltpu.SemaphoreType.DMA,

time: 184 us -> 190 us (1.033)
  Pallas kernels: 182 us -> 189 us
    pallas_call x1, Pallas kernels: 182 us -> 189 us  [shards(): pl.pallas_call(kernel, out_shape=jax.ShapeDtypeStruct((VB, 128), BF16), i...]
where the time goes in v3:
time: 190 us
  Pallas kernels  189 us (99%)
    pallas_call x1, Pallas kernels, shards(): pl.pallas_call(kernel, out_shape=jax.ShapeDtypeStruct((VB, 128), BF16), i...  189 us

profile of v3, /device:TPU:1, one launch (start us, length us, event | category | flops | bytes accessed | tf_op | source)
XLA Modules:
  0.0 190.3 jit_solution(7782378349421350809)
XLA Ops:
  0.0 188.9 %shard_map.28 = bf16[32,128]{1,0:T(8,128)(2,1)} custom-call(bf16[56,2,28672]{2,1,0:T(2,128)(2,1)} %w_ref.1, bf16[56,57344]{1,0:T(8,128)(2,1)} %t_ref.1), custom_call_target="tpu_custom_call" | custom-call | flops 12999999488 | bytes 13000000 | tf_op jit(solution)/shard_map/pallas_call | solution.py:245
  188.9 0.8 reshape.3
  189.7 0.6 copy.5

commit v4 on v2

--- a/solution.py
+++ b/solution.py
@@ -15,6 +15,7 @@
 CW = 56
 DW = 56
 VB = 32
+FAR = [(dz, dy) for dz in range(8) for dy in range(2)]
 OB = 32
 PAIRS = OB * OB
 GROUPS = 8
@@ -32,7 +33,8 @@
     u, c = r // 2, r % 2
 
     def step(g, h):
-        i = g % 4
+        n = g % 4
+        i = n + g // 4 * (3 - 2 * n + n // 2 * (2 * n - 5))
         far = (i + 3) // 4
         dz = (1 - far) * 4 * (1 - h) + far * (4 - i) * (1 - 2 * h)
         return dz, 1 - g // 4
@@ -58,7 +60,7 @@
 
     def local_copy(k):
         columns = pl.ds(pl.multiple_of(q * (DW * VB) + k * LANES, 128), LANES)
-        return pltpu.make_async_copy(w_ref.at[:, :, columns], piece(4, 1, k), w_recv.at[4, 1, k])
+        return pltpu.make_async_copy(w_ref.at[:, :, columns], piece(6, 1, k), w_recv.at[6, 1, k])
 
     t_copy = pltpu.make_async_copy(t_ref, tbuf, t_sem)
     t_copy.start()
@@ -75,7 +77,7 @@
         def _(g):
             send_piece(g, 0, slot - 2 * g).start()
 
-            @pl.when(g != 4)
+            @pl.when(g != 6)
             def _():
                 send_piece(g, 1, slot - 2 * g).start()
 
@@ -143,13 +145,12 @@
         pltpu.make_async_copy(core_in.at[g, 0], core_in.at[g, 0], core_recv.at[g, 0]).wait()
         cross_copy(g).wait_recv()
 
-        @pl.loop(1, CHIPS)
-        def _(k):
-            p = lax.rem(u + k, CHIPS)
+        for k, (dy, dx) in enumerate(((1, 2), (1, 1), (1, 3), (0, 2), (1, 0), (0, 1), (0, 3))):
+            p = lax.rem(u // 4 + dy, 2) * 4 + lax.rem(u + dx, 4)
             row_out[g, p, 0] = (acc[g, mine(p, c)] + core_in[g, 0, p]).astype(BF16)
             row_out[g, p, 1] = (cross[g, c, p] + core_in[g, 1, p]).astype(BF16)
             pltpu.make_async_remote_copy(
-                src_ref=row_out.at[g, p], dst_ref=row_in.at[g, k - 1],
+                src_ref=row_out.at[g, p], dst_ref=row_in.at[g, k],
                 send_sem=row_send.at[g], recv_sem=row_recv.at[g],
                 device_id=(p * 2 + c, q), device_id_type=MESH).start()
 
@@ -176,16 +177,19 @@
         def _(k):
             compute(g, k)
 
-            @pl.when((k == 1) & (g > 0))
-            def _():
-                pair(g - 1)
-
-            @pl.when((k == 4) & (g > 0))
-            def _():
-                collect(g - 1)
+            early = 2 * (g - GROUPS // 2)
+            for n in range(2):
+                @pl.when((k == 1 + n) & (g >= GROUPS // 2) & (early + n < GROUPS - 1))
+                def _():
+                    pair(early + n)
+
+                @pl.when((k == 4 + n) & (g >= GROUPS // 2) & (early + n < GROUPS - 2))
+                def _():
+                    collect(early + n)
 
         scatter(g)
 
+    collect(GROUPS - 2)
     pair(GROUPS - 1)
     collect(GROUPS - 1)
 
@@ -194,12 +198,12 @@
         x1 = mirror[pl.ds(2 * p + 1, 32, stride=32), :]
         return direct[p] + jnp.where(low, pltpu.roll(x0, 64, 1), x1)
 
-    @pl.loop(1, COLS, unroll=5)
-    def _(k):
-        p = lax.rem(q + k, COLS)
-        col_out[k - 1] = finish(p).astype(BF16)
+    far = [(dz, dy) for d in range(5, 0, -1) for dz, dy in FAR if min(dz, 8 - dz) + dy == d]
+    for k, (dz, dy) in enumerate(far):
+        p = lax.rem(z + dz, 8) * 2 + lax.rem(y + dy, 2)
+        col_out[k] = finish(p).astype(BF16)
         pltpu.make_async_remote_copy(
-            src_ref=col_out.at[k - 1], dst_ref=col_in.at[k - 1],
+            src_ref=col_out.at[k], dst_ref=col_in.at[k],
             send_sem=col_send, recv_sem=col_recv,
             device_id=(r, p), device_id_type=MESH).start()
 
@@ -207,7 +211,9 @@
     pltpu.make_async_copy(col_in, col_in, col_recv).wait()
     for k in range(COLS - 1):
         total += col_in[k].astype(F32)
-    o_ref[...] = total.astype(BF16)
+    for a in range(2):
+        halves = [total[:, a * 64 + i * 32:a * 64 + (i + 1) * 32] for i in range(2)]
+        o_ref[a] = jnp.stack(halves, axis=1).astype(BF16)
 
     pltpu.make_async_copy(col_out, col_out, col_send).wait()
 
@@ -218,7 +224,7 @@
         pltpu.make_async_copy(row_in.at[g], row_in.at[g], row_send.at[g]).wait()
         pltpu.make_async_copy(wbuf.at[g * 2], wbuf.at[g * 2], w_send.at[g, 0]).wait()
 
-        @pl.when(g != 4)
+        @pl.when(g != 6)
         def _():
             pltpu.make_async_copy(wbuf.at[g * 2 + 1], wbuf.at[g * 2 + 1], w_send.at[g, 1]).wait()
 
@@ -226,7 +232,7 @@
 def shards(integrals, amplitudes):
     out = pl.pallas_call(
         kernel,
-        out_shape=jax.ShapeDtypeStruct((VB, 128), BF16),
+        out_shape=jax.ShapeDtypeStruct((2, VB, 2, OB), BF16),
         in_specs=[pl.BlockSpec(memory_space=pl.ANY)] * 2,
         out_specs=pl.BlockSpec(memory_space=pltpu.VMEM),
         scratch_shapes=[
@@ -257,7 +263,7 @@
             collective_id=0, has_side_effects=True, vmem_limit_bytes=56 * 2**20),
         cost_estimate=pl.CostEstimate(flops=13 * 10**9, bytes_accessed=13 * 10**6, transcendentals=0),
     )(integrals, amplitudes)
-    return jnp.transpose(out.reshape(VB, 2, 2, OB), (1, 0, 2, 3))
+    return out
 
 
 def solution(mesh):

time: 184 us -> 170 us (0.924)
  Pallas kernels: 182 us -> 169 us
    pallas_call x1, Pallas kernels: 182 us -> 169 us  [shards(): pl.pallas_call(kernel, out_shape=jax.ShapeDtypeStruct((2, VB, 2, OB), BF1...]
where the time goes in v4:
time: 170 us
  Pallas kernels  169 us (99%)
    pallas_call x1, Pallas kernels, shards(): pl.pallas_call(kernel, out_shape=jax.ShapeDtypeStruct((2, VB, 2, OB), BF1...  169 us

profile of v4, /device:TPU:1, one launch (start us, length us, event | category | flops | bytes accessed | tf_op | source)
XLA Modules:
  0.0 170.3 jit_solution(13870083122392025703)
XLA Ops:
  0.0 168.9 %shard_map.28 = bf16[2,32,2,32]{3,2,1,0:T(2,128)(2,1)} custom-call(bf16[56,2,28672]{2,1,0:T(2,128)(2,1)} %w_ref.1, bf16[56,57344]{1,0:T(8,128)(2,1)} %t_ref.1), custom_call_target="tpu_custom_call" | custom-call | flops 12999999488 | bytes 13000000 | tf_op jit(solution)/shard_map/pallas_call | solution.py:233
  168.9 1.4 copy.4

commit v5 on v4

--- a/solution.py
+++ b/solution.py
@@ -25,7 +25,7 @@
 KP = TILES * 256
 
 
-def kernel(w_ref, t_ref, o_ref, wbuf, tbuf, lhs, rhs, acc, cross, core_in, row_out, row_in, direct, mirror,
+def kernel(w_ref, t_ref, o_ref, wbuf, tbuf, lhs, rhs, acc, core_in, row_out, row_in, direct, mirror,
            col_out, col_in, w_send, w_recv, t_sem, core_send, core_recv, row_send, row_recv, col_send, col_recv):
     r = lax.axis_index("row")
     q = lax.axis_index("col")
@@ -68,9 +68,10 @@
     barrier = pltpu.get_barrier_semaphore()
     for k in range(1, COLS):
         pl.semaphore_signal(barrier, inc=1, device_id=(r, lax.rem(q + k, COLS)), device_id_type=MESH)
-    for k in range(1, ROWS):
-        pl.semaphore_signal(barrier, inc=1, device_id=(lax.rem(r + k, ROWS), q), device_id_type=MESH)
-    pl.semaphore_wait(barrier, COLS + ROWS - 2)
+    for k in range(1, CHIPS):
+        pl.semaphore_signal(barrier, inc=1, device_id=(lax.rem(r + 2 * k, ROWS), q), device_id_type=MESH)
+    pl.semaphore_signal(barrier, inc=1, device_id=(r + 1 - 2 * c, q), device_id_type=MESH)
+    pl.semaphore_wait(barrier, COLS - 1 + CHIPS)
 
     for slot in range(2 * GROUPS + PIECES - 2):
         @pl.loop(max(0, slot - PIECES + 2) // 2, min(GROUPS - 1, slot // 2) + 1)
@@ -120,35 +121,26 @@
                     jnp.concatenate([out, pad], axis=0).astype(BF16))
         acc[g] += jnp.dot(lhs[k], rhs[...], preferred_element_type=F32)
 
-    def cross_copy(g):
+    def core_copy(g):
         return pltpu.make_async_remote_copy(
-            src_ref=cross.at[g, 1 - c], dst_ref=core_in.at[g, 1],
-            send_sem=core_send.at[g, 1], recv_sem=core_recv.at[g, 1],
+            src_ref=acc.at[g], dst_ref=core_in.at[g], send_sem=core_send.at[g], recv_sem=core_recv.at[g],
             device_id=(r + 1 - 2 * c, q), device_id_type=MESH)
 
-    def mine(p, core):
-        return pl.ds(pl.multiple_of((p * 2 + core) * 64, 64), 64)
-
-    def scatter(g):
-        @pl.loop(0, CHIPS)
-        def _(p):
-            pltpu.make_async_remote_copy(
-                src_ref=acc.at[g, mine(p, 1 - c)], dst_ref=core_in.at[g, 0, p],
-                send_sem=core_send.at[g, 0], recv_sem=core_recv.at[g, 0],
-                device_id=(r + 1 - 2 * c, q), device_id_type=MESH).start()
-
-        for j in range(OB):
-            cross[g, j // 2 % 2, j // 4, j % 2 * 32:(j % 2 + 1) * 32] = acc[g, pl.ds(j, 32, stride=32), :]
-        cross_copy(g).start()
+    def straight_cut(g, p):
+        rows = pl.ds(pl.multiple_of((p * 2 + c) * 64, 64), 64)
+        return acc[g, rows] + core_in[g, rows]
+
+    def crossed_cut(g, p, n):
+        rows = pl.ds((p * 2 + c) * 2 + n, OB, stride=OB)
+        return acc[g, rows] + core_in[g, rows]
 
     def pair(g):
-        pltpu.make_async_copy(core_in.at[g, 0], core_in.at[g, 0], core_recv.at[g, 0]).wait()
-        cross_copy(g).wait_recv()
-
+        core_copy(g).wait_recv()
         for k, (dy, dx) in enumerate(((1, 2), (1, 1), (1, 3), (0, 2), (1, 0), (0, 1), (0, 3))):
             p = lax.rem(u // 4 + dy, 2) * 4 + lax.rem(u + dx, 4)
-            row_out[g, p, 0] = (acc[g, mine(p, c)] + core_in[g, 0, p]).astype(BF16)
-            row_out[g, p, 1] = (cross[g, c, p] + core_in[g, 1, p]).astype(BF16)
+            row_out[g, p, 0] = straight_cut(g, p).astype(BF16)
+            for n in range(2):
+                row_out[g, p, 1, n * OB:(n + 1) * OB] = crossed_cut(g, p, n).astype(BF16)
             pltpu.make_async_remote_copy(
                 src_ref=row_out.at[g, p], dst_ref=row_in.at[g, k],
                 send_sem=row_send.at[g], recv_sem=row_recv.at[g],
@@ -157,8 +149,8 @@
     low = lax.broadcasted_iota(jnp.int32, (32, 128), 1) < 64
 
     def collect(g):
-        straight = acc[g, mine(u, c)] + core_in[g, 0, u]
-        crossed = cross[g, c, u] + core_in[g, 1, u]
+        straight = straight_cut(g, u)
+        crossed = jnp.concatenate([crossed_cut(g, u, n) for n in range(2)], axis=0)
         pltpu.make_async_copy(row_in.at[g], row_in.at[g], row_recv.at[g]).wait()
         for k in range(CHIPS - 1):
             straight += row_in[g, k, 0].astype(F32)
@@ -187,7 +179,7 @@
                 def _():
                     collect(early + n)
 
-        scatter(g)
+        core_copy(g).start()
 
     collect(GROUPS - 2)
     pair(GROUPS - 1)
@@ -219,8 +211,7 @@
 
     @pl.loop(0, GROUPS)
     def _(g):
-        pltpu.make_async_copy(core_in.at[g, 0], core_in.at[g, 0], core_send.at[g, 0]).wait()
-        cross_copy(g).wait_send()
+        core_copy(g).wait_send()
         pltpu.make_async_copy(row_in.at[g], row_in.at[g], row_send.at[g]).wait()
         pltpu.make_async_copy(wbuf.at[g * 2], wbuf.at[g * 2], w_send.at[g, 0]).wait()
 
@@ -241,8 +232,7 @@
             pltpu.VMEM((PIECES, PAIRS, KP), BF16),
             pltpu.VMEM((KP, 128), BF16),
             pltpu.VMEM((GROUPS, PAIRS, 128), F32),
-            pltpu.VMEM((GROUPS, 2, CHIPS, 64, 128), F32),
-            pltpu.VMEM((GROUPS, 2, CHIPS, 64, 128), F32),
+            pltpu.VMEM((GROUPS, PAIRS, 128), F32),
             pltpu.VMEM((GROUPS, CHIPS, 2, 64, 128), BF16),
             pltpu.VMEM((GROUPS, CHIPS - 1, 2, 64, 128), BF16),
             pltpu.VMEM((COLS, 32, 128), F32),
@@ -252,8 +242,8 @@
             pltpu.SemaphoreType.DMA((GROUPS, 2)),
             pltpu.SemaphoreType.DMA((GROUPS, 2, PIECES)),
             pltpu.SemaphoreType.DMA,
-            pltpu.SemaphoreType.DMA((GROUPS, 2)),
-            pltpu.SemaphoreType.DMA((GROUPS, 2)),
+            pltpu.SemaphoreType.DMA((GROUPS,)),
+            pltpu.SemaphoreType.DMA((GROUPS,)),
             pltpu.SemaphoreType.DMA((GROUPS,)),
             pltpu.SemaphoreType.DMA((GROUPS,)),
             pltpu.SemaphoreType.DMA,

time: 170 us -> 169 us (level)
  no operation moved by 1% of the time
where the time goes in v5:
time: 169 us
  Pallas kernels  168 us (99%)
    pallas_call x1, Pallas kernels, shards(): pl.pallas_call(kernel, out_shape=jax.ShapeDtypeStruct((2, VB, 2, OB), BF1...  168 us

profile of v5, /device:TPU:1, one launch (start us, length us, event | category | flops | bytes accessed | tf_op | source)
XLA Modules:
  0.0 168.9 jit_solution(4010833528670003357)
XLA Ops:
  0.0 167.5 %shard_map.28 = bf16[2,32,2,32]{3,2,1,0:T(2,128)(2,1)} custom-call(bf16[56,2,28672]{2,1,0:T(2,128)(2,1)} %w_ref.1, bf16[56,57344]{1,0:T(8,128)(2,1)} %t_ref.1), custom_call_target="tpu_custom_call" | custom-call | flops 12999999488 | bytes 13000000 | tf_op jit(solution)/shard_map/pallas_call | solution.py:224
  167.5 1.4 copy.4

commit v6 on v5

--- a/solution.py
+++ b/solution.py
@@ -18,6 +18,7 @@
 FAR = [(dz, dy) for dz in range(8) for dy in range(2)]
 OB = 32
 PAIRS = OB * OB
+SPAN = PAIRS + OB
 GROUPS = 8
 PIECES = 7
 LANES = DW * VB // PIECES
@@ -66,7 +67,7 @@
     t_copy.start()
 
     barrier = pltpu.get_barrier_semaphore()
-    for k in range(1, COLS):
+    for k in (9, 7, 8, 10, 6, 11, 5, 12, 4, 13, 3, 14, 2, 15, 1):
         pl.semaphore_signal(barrier, inc=1, device_id=(r, lax.rem(q + k, COLS)), device_id_type=MESH)
     for k in range(1, CHIPS):
         pl.semaphore_signal(barrier, inc=1, device_id=(lax.rem(r + 2 * k, ROWS), q), device_id_type=MESH)
@@ -100,7 +101,7 @@
 
     @pl.loop(0, GROUPS)
     def _(g):
-        acc[g] = jnp.zeros((PAIRS, 128), F32)
+        acc[g] = jnp.zeros((SPAN, 128), F32)
 
     quarter = lax.broadcasted_iota(jnp.int32, (CW, 128), 1) // 32
     pad = jnp.zeros((8, 128), F32)
@@ -119,11 +120,11 @@
                     out = jnp.where(quarter == n, moved, out) if n else moved
                 rhs[t * 256 + d * 64:t * 256 + (d + 1) * 64] = (
                     jnp.concatenate([out, pad], axis=0).astype(BF16))
-        acc[g] += jnp.dot(lhs[k], rhs[...], preferred_element_type=F32)
+        acc[g, :PAIRS] += jnp.dot(lhs[k], rhs[...], preferred_element_type=F32)
 
     def core_copy(g):
         return pltpu.make_async_remote_copy(
-            src_ref=acc.at[g], dst_ref=core_in.at[g], send_sem=core_send.at[g], recv_sem=core_recv.at[g],
+            src_ref=acc.at[g, pl.ds(0, PAIRS)], dst_ref=core_in.at[g, pl.ds(0, PAIRS)], send_sem=core_send.at[g], recv_sem=core_recv.at[g],
             device_id=(r + 1 - 2 * c, q), device_id_type=MESH)
 
     def straight_cut(g, p):
@@ -231,12 +232,12 @@
             pltpu.VMEM((CW, DW * PAIRS), BF16),
             pltpu.VMEM((PIECES, PAIRS, KP), BF16),
             pltpu.VMEM((KP, 128), BF16),
-            pltpu.VMEM((GROUPS, PAIRS, 128), F32),
-            pltpu.VMEM((GROUPS, PAIRS, 128), F32),
+            pltpu.VMEM((GROUPS, SPAN, 128), F32),
+            pltpu.VMEM((GROUPS, SPAN, 128), F32),
             pltpu.VMEM((GROUPS, CHIPS, 2, 64, 128), BF16),
             pltpu.VMEM((GROUPS, CHIPS - 1, 2, 64, 128), BF16),
             pltpu.VMEM((COLS, 32, 128), F32),
-            pltpu.VMEM((PAIRS, 128), F32),
+            pltpu.VMEM((SPAN, 128), F32),
             pltpu.VMEM((COLS - 1, 32, 128), BF16),
             pltpu.VMEM((COLS - 1, 32, 128), BF16),
             pltpu.SemaphoreType.DMA((GROUPS, 2)),

time: 169 us -> 169 us (level)
  no operation moved by 1% of the time
where the time goes in v6:
time: 169 us
  Pallas kernels  167 us (99%)
    pallas_call x1, Pallas kernels, shards(): pl.pallas_call(kernel, out_shape=jax.ShapeDtypeStruct((2, VB, 2, OB), BF1...  167 us

profile of v6, /device:TPU:1, one launch (start us, length us, event | category | flops | bytes accessed | tf_op | source)
XLA Modules:
  0.0 168.7 jit_solution(17365310606521477635)
XLA Ops:
  0.0 167.2 %shard_map.28 = bf16[2,32,2,32]{3,2,1,0:T(2,128)(2,1)} custom-call(bf16[56,2,28672]{2,1,0:T(2,128)(2,1)} %w_ref.1, bf16[56,57344]{1,0:T(8,128)(2,1)} %t_ref.1), custom_call_target="tpu_custom_call" | custom-call | flops 12999999488 | bytes 13000000 | tf_op jit(solution)/shard_map/pallas_call | solution.py:225
  167.3 1.4 copy.4

commit v7 on v6

--- a/solution.py
+++ b/solution.py
@@ -15,6 +15,7 @@
 CW = 56
 DW = 56
 VB = 32
+LAST = 15
 FAR = [(dz, dy) for dz in range(8) for dy in range(2)]
 OB = 32
 PAIRS = OB * OB
@@ -26,7 +27,7 @@
 KP = TILES * 256
 
 
-def kernel(w_ref, t_ref, o_ref, wbuf, tbuf, lhs, rhs, acc, core_in, row_out, row_in, direct, mirror,
+def kernel(w_ref, t_ref, o_ref, wbuf, tbuf, lhs, rhs, acc, core_in, row_out, row_in, direct, mirror, ready, turn,
            col_out, col_in, w_send, w_recv, t_sem, core_send, core_recv, row_send, row_recv, col_send, col_recv):
     r = lax.axis_index("row")
     q = lax.axis_index("col")
@@ -74,14 +75,21 @@
     pl.semaphore_signal(barrier, inc=1, device_id=(r + 1 - 2 * c, q), device_id_type=MESH)
     pl.semaphore_wait(barrier, COLS - 1 + CHIPS)
 
-    for slot in range(2 * GROUPS + PIECES - 2):
-        @pl.loop(max(0, slot - PIECES + 2) // 2, min(GROUPS - 1, slot // 2) + 1)
-        def _(g):
-            send_piece(g, 0, slot - 2 * g).start()
-
-            @pl.when(g != 6)
-            def _():
-                send_piece(g, 1, slot - 2 * g).start()
+    def send_both(g, k):
+        send_piece(g, 0, k).start()
+
+        @pl.when(g != 6)
+        def _():
+            send_piece(g, 1, k).start()
+
+    for slot in range(LAST + PIECES):
+        first, end = max(0, slot - PIECES + 2) // 2, min(GROUPS - 2, slot // 2) + 1
+        if first < end:
+            @pl.loop(first, end)
+            def _(g):
+                send_both(g, slot - 2 * g)
+        if slot >= LAST:
+            send_both(GROUPS - 1, slot - LAST)
 
     @pl.loop(0, PIECES)
     def _(k):
@@ -102,6 +110,9 @@
     @pl.loop(0, GROUPS)
     def _(g):
         acc[g] = jnp.zeros((SPAN, 128), F32)
+
+    direct[...] = jnp.zeros_like(direct)
+    mirror[...] = jnp.zeros_like(mirror)
 
     quarter = lax.broadcasted_iota(jnp.int32, (CW, 128), 1) // 32
     pad = jnp.zeros((8, 128), F32)
@@ -149,20 +160,42 @@
 
     low = lax.broadcasted_iota(jnp.int32, (32, 128), 1) < 64
 
-    def collect(g):
+    def turned(g):
         straight = straight_cut(g, u)
         crossed = jnp.concatenate([crossed_cut(g, u, n) for n in range(2)], axis=0)
         pltpu.make_async_copy(row_in.at[g], row_in.at[g], row_recv.at[g]).wait()
         for k in range(CHIPS - 1):
             straight += row_in[g, k, 0].astype(F32)
             crossed += row_in[g, k, 1].astype(F32)
-        turned = jnp.concatenate([straight, crossed], axis=0).T
+        return jnp.concatenate([straight, crossed], axis=0).T
+
+    def collect(g):
+        x = turned(g)
         for h in range(2):
             p = origin(g, h)
-            x0 = turned[h * 64:h * 64 + 32]
-            x1 = turned[h * 64 + 32:h * 64 + 64]
-            direct[p] = jnp.where(low, x0, pltpu.roll(x1, 64, 1))
-            mirror[pl.ds(pl.multiple_of(p * 64, 64), 64), :] = turned[h * 64:h * 64 + 64]
+            direct[p] = jnp.where(low, x[h * 64:h * 64 + 32], pltpu.roll(x[h * 64 + 32:h * 64 + 64], 64, 1))
+            mirror[pl.ds(pl.multiple_of(p * 64, 64), 64), :] = x[h * 64:h * 64 + 64]
+
+    def tile(p):
+        return pl.ds(pl.multiple_of(p * VB, VB), VB)
+
+    def merge():
+        @pl.loop(0, COLS, unroll=4)
+        def _(p):
+            x0 = mirror[pl.ds(2 * p, 32, stride=32), :]
+            x1 = mirror[pl.ds(2 * p + 1, 32, stride=32), :]
+            ready[tile(p), :] = direct[p] + jnp.where(low, pltpu.roll(x0, 64, 1), x1)
+
+    def collect_last(g):
+        x = turned(g)
+        turn[:128] = x
+        for h in range(2):
+            p = origin(g, h)
+            ready[tile(p), :] += jnp.where(low, x[h * 64:h * 64 + 32], pltpu.roll(x[h * 64 + 32:h * 64 + 64], 64, 1))
+            for a in range(2):
+                x0 = turn[pl.ds(h * 64 + a * 32, COLS, stride=2), :]
+                x1 = turn[pl.ds(h * 64 + a * 32 + 1, COLS, stride=2), :]
+                ready[pl.ds(2 * p + a, COLS, stride=VB), :] += jnp.where(low[:COLS], pltpu.roll(x0, 64, 1), x1)
 
     @pl.loop(0, GROUPS)
     def _(g):
@@ -184,23 +217,19 @@
 
     collect(GROUPS - 2)
     pair(GROUPS - 1)
-    collect(GROUPS - 1)
-
-    def finish(p):
-        x0 = mirror[pl.ds(2 * p, 32, stride=32), :]
-        x1 = mirror[pl.ds(2 * p + 1, 32, stride=32), :]
-        return direct[p] + jnp.where(low, pltpu.roll(x0, 64, 1), x1)
+    merge()
+    collect_last(GROUPS - 1)
 
     far = [(dz, dy) for d in range(5, 0, -1) for dz, dy in FAR if min(dz, 8 - dz) + dy == d]
     for k, (dz, dy) in enumerate(far):
         p = lax.rem(z + dz, 8) * 2 + lax.rem(y + dy, 2)
-        col_out[k] = finish(p).astype(BF16)
+        col_out[k] = ready[tile(p), :].astype(BF16)
         pltpu.make_async_remote_copy(
             src_ref=col_out.at[k], dst_ref=col_in.at[k],
             send_sem=col_send, recv_sem=col_recv,
             device_id=(r, p), device_id_type=MESH).start()
 
-    total = finish(q)
+    total = ready[tile(q), :]
     pltpu.make_async_copy(col_in, col_in, col_recv).wait()
     for k in range(COLS - 1):
         total += col_in[k].astype(F32)
@@ -238,6 +267,8 @@
             pltpu.VMEM((GROUPS, CHIPS - 1, 2, 64, 128), BF16),
             pltpu.VMEM((COLS, 32, 128), F32),
             pltpu.VMEM((SPAN, 128), F32),
+            pltpu.VMEM((COLS * VB + VB, 128), F32),
+            pltpu.VMEM((128 + 2, 128), F32),
             pltpu.VMEM((COLS - 1, 32, 128), BF16),
             pltpu.VMEM((COLS - 1, 32, 128), BF16),
             pltpu.SemaphoreType.DMA((GROUPS, 2)),

time: 169 us -> 169 us (level)
  no operation moved by 1% of the time
where the time goes in v7:
time: 169 us
  Pallas kernels  167 us (99%)
    pallas_call x1, Pallas kernels, shards(): pl.pallas_call(kernel, out_shape=jax.ShapeDtypeStruct((2, VB, 2, OB), BF1...  167 us

profile of v7, /device:TPU:1, one launch (start us, length us, event | category | flops | bytes accessed | tf_op | source)
XLA Modules:
  0.0 168.5 jit_solution(7692491196357924815)
XLA Ops:
  0.0 167.1 %shard_map.28 = bf16[2,32,2,32]{3,2,1,0:T(2,128)(2,1)} custom-call(bf16[56,2,28672]{2,1,0:T(2,128)(2,1)} %w_ref.1, bf16[56,57344]{1,0:T(8,128)(2,1)} %t_ref.1), custom_call_target="tpu_custom_call" | custom-call | flops 12999999488 | bytes 13000000 | tf_op jit(solution)/shard_map/pallas_call | solution.py:254
  167.1 1.4 copy.4
